TPU v7x, 32 devices: a whole 2x2x4 slice. The times are simulated.
32 devices in a mesh: idx: 8 (over z, y), tp: 4 (over x, core).
Axes of the slice: x: 2, y: 2, z: 4, core: 2. Of those that a mesh axis runs over, the one named last changes fastest.
Arguments:
- activations: bfloat16 [8192, 28672], P('idx', 'tp'), may hold values from -6 to 6
- out_grads: bfloat16 [8192, 8192], P('idx', 'tp'), may hold values from -6 to 6
- proj_in: bfloat16 [28672, 64], P('tp'), may hold values from -0.03125 to 0.03125
- proj_out: bfloat16 [8192, 64], P('tp'), may hold values from -0.0625 to 0.0625
- doc_ids: int32 [8192], P('idx'), may hold values from 0 to 1023, never falling along the last dimension, each value on 1 to 32 neighbouring positions
- doc_order: int32 [1024], replicated, may hold values from 0 to 1023, each once
- inv_fisher: float32 [4096, 4096], P('tp'), may hold values from -1 to 3, as said below
- index_grads: bfloat16 [32768, 4096], P(('idx', 'tp')), may hold values from -0.0234375 to 0.0234375
Outputs:
- scores: float32 [1024, 32768], P(None, ('idx', 'tp'))
Inputs may be any that keep to these rules, and one draw needn't show every extreme that they name: `inv_fisher`: an estimate of the inverse Fisher of the projected gradients.
All inputs are finite; a program needn't handle non-finite values.
Results may differ from a plain program's by a relative error of at most 0.0029.
Values may be sent and summed in bfloat16 or wider, within the bound.
No kernel may reach another device: no remote copies, remote signals or barrier semaphores. Data moves between devices by JAX's collectives and lax.ppermute only.
A program may use at most 128 MiB of HBM per device.

v0:
```python
import jax
import jax.numpy as jnp
from jax import lax
from jax.sharding import PartitionSpec as P


def per_device(
    activations, out_grads, proj_in, proj_out, doc_ids, doc_order, inv_fisher, index_grads
):
    part_in = jnp.dot(activations, proj_in, preferred_element_type=jnp.float32)
    part_out = jnp.dot(out_grads, proj_out, preferred_element_type=jnp.float32)
    proj_acts, proj_grads = lax.psum((part_in, part_out), "tp")
    rank_width = proj_acts.shape[1]
    feature_width = inv_fisher.shape[0]
    lead_count = feature_width // rank_width
    grad_slice = lax.dynamic_slice_in_dim(
        proj_grads, lax.axis_index("tp") * lead_count, lead_count, 1
    )
    token_grads = (grad_slice[:, :, None] * proj_acts[:, None, :]).reshape(
        grad_slice.shape[0], feature_width
    )
    membership = (doc_ids[:, None] == doc_order[None, :]).astype(jnp.float32)
    partial_value = lax.dot_general(
        membership,
        token_grads,
        (((0,), (0,)), ((), ())),
        precision=lax.Precision.HIGHEST,
        preferred_element_type=jnp.float32,
    )
    owned_rows = lax.psum_scatter(partial_value, "idx", scatter_dimension=0, tiled=True)
    shares = lax.psum_scatter(
        jnp.dot(
            owned_rows,
            inv_fisher,
            precision=lax.Precision.HIGHEST,
            preferred_element_type=jnp.float32,
        ),
        "tp",
        scatter_dimension=0,
        tiled=True,
    )
    queries = shares.astype(jnp.bfloat16)
    return lax.dot_general(
        lax.all_gather(queries, ("idx", "tp"), axis=0, tiled=True),
        index_grads,
        (((1,), (1,)), ((), ())),
        preferred_element_type=jnp.float32,
    )


def solution(mesh):
    placed = (
        P("idx", "tp"),
        P("idx", "tp"),
        P("tp", None),
        P("tp", None),
        P("idx"),
        P(),
        P("tp", None),
        P(("idx", "tp"), None),
    )
    return jax.shard_map(
        per_device, mesh=mesh, in_specs=placed, out_specs=P(None, ("idx", "tp")), check_vma=False
    )
```

profile of v0, /device:TPU:0, one launch (start us, length us, event | category | flops | bytes accessed | tf_op | source)
XLA Modules:
  0.0 303.8 jit_solution(5826010885977179144)
XLA Ops:
  6.5 0.0 copy-start
  6.5 0.0 copy-start.3
  6.5 0.0 all-reduce.3.cloned.1.call-start
  6.5 1.2 copy-done
  7.7 0.0 copy-start.2
  7.7 10.6 %fusion.4 = f32[1024,64]{0,1:T(8,128)} fusion(bf16[1024,7168]{1,0:T(8,128)(2,1)} %param.8, bf16[7168,64]{0,1:T(8,128)(2,1)S(1)} %copy-done), kind=kOutput, calls=%fused_computation.7 | convolution fusion | flops 939524096 | bytes 15859712 | tf_op jit(solution)/shard_map/dot_general | solution.py:10
  18.3 0.0 copy-done.3
  18.3 0.0 copy-done.2
  18.3 0.0 copy-start.4
  18.3 0.0 copy-start.5
  18.3 2.1 fusion.3
  20.4 0.0 all-reduce.3.cloned.1.call-update
  20.4 0.0 reduce-scatter.3.cloned.1.call-start
  20.5 36.0 %all-reduce.3.cloned.1.call-done = (f32[1024,64]{0,1:T(8,128)}, f32[1024,64]{0,1:T(8,128)}) async-done(((f32[1024,64]{0,1:T(8,128)}, f32[1024,64]{0,1:T(8,128)}), (f32[1024,64]{0,1:T(8,128)}, f32[1024,64]{0,1:T(8,128)})) %all-reduce.3.cloned.1.call-update) | async-done | bytes 524304 | tf_op jit(solution)/shard_map/psum | solution.py:12
  56.5 0.8 constant_dynamic-slice_fusion
  57.3 1.5 broadcast_multiply_fusion
  58.8 0.0 copy-done.4
  58.8 0.0 copy-done.5
  58.9 10.0 %fusion = f32[1024,1024]{1,0:T(8,128)} fusion(f32[1024,1024]{0,1:T(8,128)S(1)} %bitcast.10, s32[1024]{0:T(1024)S(1)} %copy-done.4, s32[1024]{0:T(1024)S(1)} %copy-done.5), kind=kOutput, calls=%fused_computation.1 | convolution fusion | flops 12886999040 | bytes 8396800 | tf_op jit(solution)/shard_map/dot_general | solution.py:23
  68.8 0.0 reduce-scatter.3.cloned.1.call-update
  68.8 0.2 reduce-scatter.5.cloned.1.call-start
  69.1 88.0 %reduce-scatter.3.cloned.1.call-done = f32[128,1024]{1,0:T(8,128)} async-done(((f32[1024,1024]{1,0:T(8,128)}), f32[128,1024]{1,0:T(8,128)}) %reduce-scatter.3.cloned.1.call-update) | async-done | bytes 524304 | tf_op jit(solution)/shard_map/reduce_scatter | solution.py:30
  157.1 13.5 %fusion.5 = f32[128,4096]{1,0:T(8,128)} fusion(f32[128,1024]{1,0:T(8,128)} %reduce-scatter.3.cloned.1.call-done, f32[1024,4096]{1,0:T(8,128)} %param.14), kind=kOutput, calls=%fused_computation.8 | convolution fusion | flops 6442450944 | bytes 19398656 | tf_op jit(solution)/shard_map/dot_general | solution.py:32
  170.5 0.0 reduce-scatter.5.cloned.1.call-update
  170.6 0.0 all-gather.2.cloned.1.call-start
  170.6 31.3 %reduce-scatter.5.cloned.1.call-done = f32[32,4096]{1,0:T(8,128)} async-done(((f32[128,4096]{1,0:T(8,128)}), f32[32,4096]{1,0:T(8,128)}) %reduce-scatter.5.cloned.1.call-update) | async-done | bytes 524304 | tf_op jit(solution)/shard_map/reduce_scatter | solution.py:31
  201.9 1.8 convert_element_type.4
  203.7 0.0 all-gather.2.cloned.1.call-update
  203.7 78.4 %all-gather.2.cloned.1.call-done = bf16[1024,4096]{1,0:T(8,128)(2,1)} async-done(((bf16[32,4096]{1,0:T(8,128)(2,1)}), bf16[1024,4096]{1,0:T(8,128)(2,1)}) %all-gather.2.cloned.1.call-update) | async-done | bytes 8388624 | tf_op jit(solution)/shard_map/all_gather | solution.py:44
  282.1 0.0 copy-start.1
  282.1 15.1 %fusion.6 = f32[1024,1024]{1,0:T(8,128)} fusion(bf16[1024,4096]{1,0:T(8,128)(2,1)} %all-gather.2.cloned.1.call-done, bf16[1024,4096]{1,0:T(8,128)(2,1)} %param.15), kind=kOutput, calls=%fused_computation.9 | convolution fusion | flops 8589934592 | bytes 20971520 | tf_op jit(solution)/shard_map/dot_general | solution.py:43
  297.2 0.0 copy-done.1
Async XLA Ops:
  6.5 1.2 copy-start
  6.5 11.8 %copy-start.3 = (bf16[2048,64]{0,1:T(8,128)(2,1)S(1)}, bf16[2048,64]{0,1:T(8,128)(2,1)}, u32[]{:S(2)}) copy-start(bf16[2048,64]{0,1:T(8,128)(2,1)} %param.11) | copy-start | bytes 786436
  6.5 50.0 %all-reduce.3.cloned.1.call-start = ((), (), s32[]{:S(2)}) async-start(), calls=%async_computation.5 | async-start | bytes 1048576 | tf_op jit(solution)/shard_map/psum | solution.py:12
  7.7 10.6 %copy-start.2 = (bf16[1024,2048]{1,0:T(8,128)(2,1)S(1)}, bf16[1024,2048]{1,0:T(8,128)(2,1)}, u32[]{:S(2)}) copy-start(bf16[1024,2048]{1,0:T(8,128)(2,1)} %param.9) | copy-start | bytes 12582916
  18.3 40.5 %copy-start.4 = (s32[1024]{0:T(1024)S(1)}, s32[1024]{0:T(1024)}, u32[]{:S(2)}) copy-start(s32[1024]{0:T(1024)} %param.13) | copy-start | bytes 12292
  18.3 40.5 %copy-start.5 = (s32[1024]{0:T(1024)S(1)}, s32[1024]{0:T(1024)}, u32[]{:S(2)}) copy-start(s32[1024]{0:T(1024)} %param.12) | copy-start | bytes 12292
  20.4 136.6 %reduce-scatter.3.cloned.1.call-start = ((), (), s32[]{:S(2)}) async-start(), calls=%async_computation.2 | async-start | bytes 4718592 | tf_op jit(solution)/shard_map/reduce_scatter | solution.py:30
  68.8 133.1 %reduce-scatter.5.cloned.1.call-start = ((), (), s32[]{:S(2)}) async-start(), calls=%async_computation.3 | async-start | bytes 2621440 | tf_op jit(solution)/shard_map/reduce_scatter | solution.py:31
  170.6 111.6 %all-gather.2.cloned.1.call-start = ((), (), s32[]{:S(2)}) async-start(), calls=%async_computation.4 | async-start | bytes 8650752 | tf_op jit(solution)/shard_map/all_gather | solution.py:44
  282.1 15.1 %copy-start.1 = (bf16[7168,64]{0,1:T(8,128)(2,1)S(1)}, bf16[7168,64]{0,1:T(8,128)(2,1)}, u32[]{:S(2)}) copy-start(bf16[7168,64]{0,1:T(8,128)(2,1)} %param.10) | copy-start | bytes 2752516
Sparse Core Ops, SparseCore 0:
  20.6 35.8 all-reduce.2
  69.0 88.0 reduce-scatter.2
  170.7 31.1 reduce-scatter.4
  204.6 77.4 all-gather.1
where the time goes:
time: 304 us
  waiting for transfers between devices  234 us (77%)
  matrix products  51.2 us (17%)
  between operations  13.2 us (4%)
  other arithmetic  3.25 us (1%)
    reduce_scatter x1, waiting for transfers between devices, per_device(): lax.psum_scatter(partial_value, 'idx', scatter_dimension=0, tiled=True)  88 us
    all_gather x1, waiting for transfers between devices, per_device(): lax.all_gather(queries, ('idx', 'tp'), axis=0, tiled=True)  78.4 us
    psum x1, waiting for transfers between devices, per_device(): proj_acts, proj_grads = lax.psum((part_in, part_out), 'tp')  36 us
    reduce_scatter x1, waiting for transfers between devices, per_device(): lax.psum_scatter(jnp.dot(owned_rows, inv_fisher, precision=lax.Precision....  31.3 us
    dot_general x1, matrix products, per_device(): lax.dot_general(lax.all_gather(queries, ('idx', 'tp'), axis=0, tiled=True...  15.1 us
    dot_general x1, matrix products, per_device(): jnp.dot(owned_rows, inv_fisher, precision=lax.Precision.HIGHEST, preferre...  13.5 us
    dot_general x1, matrix products, per_device(): part_in = jnp.dot(activations, proj_in, preferred_element_type=jnp.float32)  10.6 us
    dot_general x1, matrix products, per_device(): lax.dot_general(membership, token_grads, (((0,), (0,)), ((), ())), precis...  9.96 us
  transfers between devices with their start and end apart: 4, of which 4 were waited for; matrix products, arithmetic and copies ran while one was open for 0% of the time, Pallas kernels for 0%

commit v1 on v0

v1 whole, which is shorter than its diff:
```python
import functools

import jax
import jax.numpy as jnp
from jax import lax
from jax.experimental import pallas as pl
from jax.experimental.pallas import tpu as pltpu
from jax.sharding import PartitionSpec as P

AXES = ("idx", "tp")
F32, BF16 = jnp.float32, jnp.bfloat16
MIB = 1024 * 1024
IN_SMEM = pl.BlockSpec(memory_space=pltpu.SMEM)
IN_VMEM = pl.BlockSpec(memory_space=pltpu.VMEM)


def across(a, b):
    return lax.dot_general(a, b, (((1,), (1,)), ((), ())), preferred_element_type=F32)


def project(core_ref, acts_ref, grads_ref, in_ref, out_ref, keep_ref, send_ref):
    step = pl.program_id(0)
    rank, tokens = in_ref.shape[0], acts_ref.shape[0]
    blocks = keep_ref.shape[1] // tokens
    place = pl.ds(pl.multiple_of(lax.rem(step, blocks) * tokens, tokens), tokens)
    acts = across(acts_ref[...], in_ref[...]).T
    grads = across(grads_ref[...], out_ref[...]).T
    mine = step // blocks == core_ref[0]

    @pl.when(mine)
    def _():
        keep_ref[:rank, place] = acts
        keep_ref[rank:, place] = grads

    @pl.when(jnp.logical_not(mine))
    def _():
        send_ref[:rank, place] = acts
        send_ref[rank:, place] = grads


def split(value):
    high = value.astype(BF16)
    return high, (value - high.astype(F32)).astype(BF16)


def condition(parts, lead, first_ref, *refs):
    parts_refs = refs[:parts]
    fisher_ref, keep_ref, send_ref, fisher, sums, arrived = refs[parts:]
    blocks, depth, width = fisher.shape

    def fetch(b):
        return pltpu.make_async_copy(
            fisher_ref.at[:, pl.ds(b * width, width)], fisher.at[b], arrived.at[b]
        )

    for b in range(blocks):
        fetch(b).start()
    documents = sums.shape[0] // 2
    rank, tokens = sums.shape[1] // lead, parts_refs[0].shape[1]
    core = first_ref[1]
    own = (first_ref[0] + lax.broadcasted_iota(jnp.int32, (documents, tokens), 0)).astype(F32)
    last = rank + 2 * lead
    members = [(own == ref[last : last + 1, :]).astype(F32).astype(BF16) for ref in parts_refs]
    leads = [
        jnp.where(core == 0, ref[rank : rank + lead, :], ref[rank + lead : last, :])
        for ref in parts_refs
    ]
    for i in range(0, lead, 2):
        total = None
        for member, ref, grads in zip(members, parts_refs, leads, strict=True):
            acts = ref[:rank, :]
            value = jnp.concatenate([grads[i : i + 1, :] * acts, grads[i + 1 : i + 2, :] * acts])
            high, low = split(value)
            term = across(member, high) + across(member, low)
            total = term if total is None else total + term
        high, low = split(total)
        sums[:documents, i * rank : (i + 2) * rank] = high
        sums[documents:, i * rank : (i + 2) * rank] = low
    rows = documents // 2
    for b in range(blocks):
        fetch(b).wait()
        high, low = split(fisher[b])
        both = jnp.dot(sums[...], high, preferred_element_type=F32)
        value = both[:documents] + both[documents:] + jnp.dot(
            sums[:documents, :], low, preferred_element_type=F32
        )
        columns = slice(b * width, (b + 1) * width)
        keep_ref[:, columns] = jnp.where(core == 0, value[:rows], value[rows:])
        send_ref[:, columns] = jnp.where(core == 0, value[rows:], value[:rows])


def score(pieces, *refs):
    index_ref, out_ref, stacked = refs[pieces:]
    base = 0
    for ref in refs[:pieces]:
        stacked[base : base + ref.shape[0], :] = ref[...]
        base += ref.shape[0]
    columns = out_ref.shape[1]
    block = min(256, columns)
    for c in range(0, columns, block):
        out_ref[:, c : c + block] = across(stacked[...], index_ref[c : c + block, :])


def place_rows(dest_ref, *refs):
    out_ref = refs[-1]
    base = 0
    for ref in refs[:-1]:

        def body(group, carry, ref=ref, base=base):
            start = group * 8
            rows = [ref[pl.ds(start + k, 1), :] for k in range(8)]
            for k, row in enumerate(rows):
                out_ref[pl.ds(dest_ref[base + start + k], 1), :] = row
            return carry

        lax.fori_loop(0, ref.shape[0] // 8, body, 0)
        base += ref.shape[0]


def solution(mesh):
    n_idx, n_tp = mesh.shape["idx"], mesh.shape["tp"]
    n_x = n_tp // 2
    n_y = 2 if n_idx % 2 == 0 else 1
    n_z = n_idx // n_y
    box = n_x == 2 and n_y == 2 and n_z == 4

    def pattern(move):
        pairs = []
        for g in range(n_idx):
            for x in range(n_x):
                for c in range(2):
                    to = move(g, x, c)
                    if 0 <= to[0] < n_idx:
                        pairs.append(((g * n_x + x) * 2 + c, (to[0] * n_x + to[1]) * 2 + to[2]))
        return pairs

    to_core = pattern(lambda g, x, c: (g, x, 1 - c))
    to_next = pattern(lambda g, x, c: (g + 1, x, 0) if c == 1 else (g - 1, x, 1))
    ring = pattern(lambda g, x, c: ((g + 1) % n_idx, x, c))
    to_plane = pattern(lambda g, x, c: (g, x ^ 1, c) if c == 0 else (g ^ 1, x, c))
    to_line = pattern(lambda g, x, c: ((g + n_y * (1 - 2 * c)) % n_idx, x, c))

    def to_x(step):
        return pattern(lambda g, x, c: (g, x ^ step, c))

    steps = []
    step = n_x // 2
    while step >= 1:
        steps.append(step)
        step //= 2

    def send(value, pairs):
        return lax.ppermute(value, AXES, pairs)

    def send_all(values, pairs):
        return [send(v, pairs) for v in values]

    def cut(value, index, size, axis):
        return lax.dynamic_slice_in_dim(value, index * size, size, axis)

    def per_device(
        activations, out_grads, proj_in, proj_out, doc_ids, doc_order, inv_fisher, index_grads
    ):
        g, tp = lax.axis_index("idx"), lax.axis_index("tp")
        x, core = tp // 2, tp % 2
        rank = proj_in.shape[1]
        lead = rank // n_tp
        tokens, hidden = activations.shape
        features = out_grads.shape[1]
        half = tokens // 2
        documents = doc_order.shape[0]
        own_docs = documents // n_idx
        piece = own_docs // n_tp
        depth, width = inv_fisher.shape
        columns = index_grads.shape[0]

        block = min(256, half)
        out_half = jax.ShapeDtypeStruct((2 * rank, half), F32)
        keep, give = pl.pallas_call(
            project,
            grid=(tokens // block,),
            in_specs=[
                IN_SMEM,
                pl.BlockSpec((block, hidden), lambda s: (s, 0)),
                pl.BlockSpec((block, features), lambda s: (s, 0)),
                pl.BlockSpec((rank, hidden), lambda s: (0, 0)),
                pl.BlockSpec((rank, features), lambda s: (0, 0)),
            ],
            out_specs=[pl.BlockSpec((2 * rank, half), lambda s: (0, 0))] * 2,
            out_shape=[out_half, out_half],
            compiler_params=pltpu.CompilerParams(vmem_limit_bytes=58 * MIB),
        )(core[None], activations, out_grads, proj_in.T, proj_out.T)
        mine = keep + send(give, to_core)
        for step in steps:
            bit = (x // step) % 2
            rows = (mine.shape[0] - rank) // 2

            def half_of(b, mine=mine, rows=rows):
                return jnp.concatenate([mine[:rank], cut(mine[rank:], b, rows, 0)])

            mine = half_of(bit) + send(half_of(1 - bit), to_x(step))

        ids = jnp.broadcast_to(cut(doc_ids, core, half, 0).astype(F32)[None], (8, half))
        own_part = jnp.concatenate([mine, ids])
        parts = [own_part, send(own_part, to_next)]
        parts += send_all(parts, to_core)

        group = doc_ids // own_docs
        far = (
            (group[0] < g - 1) | (group[half - 1] > g) | (group[half] < g) | (group[-1] > g + 1)
        )

        def conditioned(parts):
            blocks = 8
            out_half = jax.ShapeDtypeStruct((own_docs // 2, width), F32)
            return pl.pallas_call(
                functools.partial(condition, len(parts), lead),
                in_specs=[IN_SMEM]
                + [IN_VMEM] * len(parts)
                + [pl.BlockSpec(memory_space=pl.ANY)],
                out_specs=[IN_VMEM] * 2,
                out_shape=[out_half, out_half],
                scratch_shapes=[
                    pltpu.VMEM((blocks, depth, width // blocks), F32),
                    pltpu.VMEM((2 * own_docs, depth), BF16),
                    pltpu.SemaphoreType.DMA((blocks,)),
                ],
                compiler_params=pltpu.CompilerParams(vmem_limit_bytes=40 * MIB),
            )(
                jnp.stack([g * own_docs, core]),
                *parts,
                inv_fisher,
            )

        def exchange(value, pairs):
            scale = jnp.max(jnp.abs(value), axis=1, keepdims=True)
            scale = jnp.where(scale > 0, scale, 1.0)
            there = send((value / scale).astype(jnp.float16), pairs)
            scale = send(jnp.broadcast_to(scale, (value.shape[0], 128)), pairs)
            return there.astype(F32) * scale[:, :1]

        def own_queries(keep, give):
            partial = keep + send(give, to_core)
            rows = own_docs // 2
            for step in steps:
                bit = (x // step) % 2
                rows //= 2
                partial = cut(partial, bit, rows, 0) + exchange(
                    cut(partial, 1 - bit, rows, 0), to_x(step)
                )
            return partial

        def gather(q):
            if not box:
                everything = lax.all_gather(q, AXES, axis=0, tiled=True)
                origin = [(h, t // 2, t % 2) for h in range(n_idx) for t in range(n_tp)]
                return [[everything]], origin, [everything[h * own_docs :] for h in range(n_idx)]
            own = [q, send(q, to_core)]
            line = send_all(own, to_line)
            plane0 = send_all(own, to_plane)
            other0 = send_all(plane0, to_core)
            corner0 = [send(other0[1], to_plane)]
            corner0 += send_all(corner0, to_core)
            two = [send(line[0], to_line)]
            off = send_all(line, to_core)
            plane1 = send_all(line, to_plane)
            two += send_all(two, to_core)
            plane2 = send_all(off, to_plane)
            corner1 = send_all(corner0, to_line)
            plane3 = send_all(two, to_plane)
            other1, other2 = send_all(plane1, to_core), send_all(plane2, to_core)
            corner3 = [send(corner1[0], to_line)]
            corner2 = send_all(corner1, to_core)
            other3 = send_all(plane3, to_core)
            corner3 += send_all(corner3, to_core)

            there = 1 - 2 * core
            below, above, opposite = [(g + d * n_y) % n_idx for d in (-there, there, 2)]
            mates = ((x ^ 1, 0), (x, 1))
            near_x, near_y = [jnp.where(core == 0, mates[0][i], mates[1][i]) for i in (0, 1)]
            far_x, far_y = [jnp.where(core == 0, mates[1][i], mates[0][i]) for i in (0, 1)]

            def level(h, swapped):
                here = [core, 1 - core]
                near_labels = here[::-1] if swapped else here
                other_labels = here[::-1]
                return (
                    [(h, x, c) for c in near_labels]
                    + [(h ^ near_y, near_x, c) for c in near_labels]
                    + [(h ^ far_y, far_x, c) for c in other_labels[:: -1 if swapped else 1]]
                    + [(h ^ 1, x ^ 1, c) for c in near_labels]
                )

            batches = [
                own + plane0 + other0 + corner0,
                line + plane1 + other2 + corner1,
                off + plane2 + other1 + corner2,
                two + plane3 + other3 + corner3,
            ]
            origin = level(g, False)
            line_level, off_level = level(below, False), level(above, True)
            line_level[4:6], off_level[4:6] = (
                [(h, xx, c) for (h, xx, _), c in zip(line_level[4:6], (core, 1 - core))],
                [(h, xx, c) for (h, xx, _), c in zip(off_level[4:6], (1 - core, core))],
            )
            return batches, origin + line_level + off_level + level(opposite, False), [
                p[0] for p in (own, line, off, two, corner0, corner1, corner2, corner3)
            ]

        def scores_of(batch):
            pieces = len(batch)
            rows = sum(b.shape[0] for b in batch)
            block = min(256, columns)
            return pl.pallas_call(
                functools.partial(score, pieces),
                in_specs=[IN_VMEM] * (pieces + 1),
                out_specs=IN_VMEM,
                out_shape=jax.ShapeDtypeStruct((rows, columns), F32),
                scratch_shapes=[pltpu.VMEM((rows, width), BF16)],
                compiler_params=pltpu.CompilerParams(vmem_limit_bytes=24 * MIB),
                cost_estimate=pl.CostEstimate(
                    flops=2 * rows * columns * width,
                    bytes_accessed=2 * width * columns + 4 * rows * columns,
                    transcendentals=0,
                ),
            )(*batch, index_grads)

        def place(scores, dest):
            return pl.pallas_call(
                place_rows,
                out_shape=jax.ShapeDtypeStruct((documents, columns), F32),
                in_specs=[IN_SMEM] + [IN_VMEM] * len(scores),
                out_specs=IN_VMEM,
                compiler_params=pltpu.CompilerParams(vmem_limit_bytes=32 * MIB),
            )(dest, *scores)

        def rows_of(origin):
            first = jnp.stack([h * own_docs + c * (own_docs // 2) + xx * piece for h, xx, c in origin])
            docs = (first[:, None] + jnp.arange(piece, dtype=jnp.int32)[None, :]).reshape(-1)
            order = jnp.arange(documents, dtype=jnp.int32)[None, :]
            return jnp.sum(jnp.where(docs[:, None] == doc_order[None, :], order, 0), axis=1)

        q = own_queries(*conditioned(parts))
        batches, origin, seen = gather(jnp.where(far, jnp.nan, q).astype(BF16))
        probe = functools.reduce(jnp.add, [p[:8, :128].astype(F32) for p in seen])
        any_far = jnp.isnan(probe[0, 0])
        dest = rows_of(origin)
        scores = [scores_of(b) for b in batches]

        def near(_):
            return place(scores, dest)

        def everywhere(_):
            block = [parts[0], parts[2]]
            total = conditioned(block)

            def body(_, carry):
                block, total = carry
                block = send_all(block, ring)
                return block, [a + b for a, b in zip(total, conditioned(block))]

            _, total = lax.fori_loop(0, n_idx - 1, body, (block, list(total)))
            batches, _, _ = gather(own_queries(*total).astype(BF16))
            return place([scores_of(b) for b in batches], dest)

        return lax.cond(any_far, everywhere, near, 0)

    placed = (
        P("idx", "tp"),
        P("idx", "tp"),
        P("tp", None),
        P("tp", None),
        P("idx"),
        P(),
        P("tp", None),
        P(("idx", "tp"), None),
    )
    return jax.shard_map(
        per_device, mesh=mesh, in_specs=placed, out_specs=P(None, ("idx", "tp")), check_vma=False
    )
```

time: 304 us -> 133 us (0.44)
  waiting for transfers between devices: 234 us -> 34.8 us
  matrix products: 51.2 us -> 0 us
  Pallas kernels: 0 us -> 49.6 us
  starting transfers between devices: 0.31 us -> 35.7 us
  between operations: 13.2 us -> 4.08 us
  local copies, waits for them, and re-layouts: 2.04 us -> 6.33 us
    reduce_scatter x2 -> x0, waiting for transfers between devices: 119 us -> none  [the longest x1 88 us: per_device(): lax.psum_scatter(partial_value, 'idx', scatter_dimension=0, tiled=True)]
    all_gather x1 -> x0, waiting for transfers between devices: 78.4 us -> none  [per_device(): lax.all_gather(queries, ('idx', 'tp'), axis=0, tiled=True)]
    dot_general x5 -> x0, matrix products: 51.2 us -> none  [the longest x1 15.1 us: per_device(): lax.dot_general(lax.all_gather(queries, ('idx', 'tp'), axis=0, tiled=True...]
    pallas_call x0 -> x7, Pallas kernels: none -> 49.6 us  [the longest x4 23.6 us: scores_of(): pl.pallas_call(functools.partial(score, pieces), in_specs=[IN_VMEM] * (pi...]
    psum x1 -> x0, waiting for transfers between devices: 36 us -> none  [per_device(): proj_acts, proj_grads = lax.psum((part_in, part_out), 'tp')]
    ppermute x0 -> x39, starting transfers between devices: none -> 35.7 us  [send(): return lax.ppermute(value, AXES, pairs)]
    ppermute x0 -> x39, waiting for transfers between devices: none -> 34.8 us  [send(): return lax.ppermute(value, AXES, pairs)]
    unnamed x12 -> x24, local copies, waits for them, and re-layouts: 1.19 us -> 4.97 us
  transfers between devices with their start and end apart: 4 -> 39, of which waited for: 4 -> 16; matrix products, arithmetic and copies ran while one was open for 0% -> 2% of each run, Pallas kernels for 0% -> 13%
where the time goes in v1:
time: 133 us
  Pallas kernels  49.6 us (37%)
  starting transfers between devices  35.7 us (27%)
  waiting for transfers between devices  34.8 us (26%)
  local copies, waits for them, and re-layouts  6.33 us (5%)
  between operations  4.08 us (3%)
  other arithmetic  2.62 us (2%)
    ppermute x39, starting transfers between devices, send(): return lax.ppermute(value, AXES, pairs)  35.7 us
    ppermute x39, waiting for transfers between devices, send(): return lax.ppermute(value, AXES, pairs)  34.8 us
    pallas_call x4, Pallas kernels, scores_of(): pl.pallas_call(functools.partial(score, pieces), in_specs=[IN_VMEM] * (pi...  23.6 us
    pallas_call x1, Pallas kernels, per_device(): pl.pallas_call(project, grid=(tokens // block,), in_specs=[IN_SMEM, pl.Bl...  10.3 us
    pallas_call x1, Pallas kernels, conditioned(): pl.pallas_call(functools.partial(condition, len(parts), lead), in_specs=[...  9.3 us
    pallas_call x1, Pallas kernels, place(): pl.pallas_call(place_rows, out_shape=jax.ShapeDtypeStruct((documents, col...  6.41 us
    unnamed x24, local copies, waits for them, and re-layouts  4.97 us
  transfers between devices with their start and end apart: 39, of which 16 were waited for; matrix products, arithmetic and copies ran while one was open for 2% of the time, Pallas kernels for 13%

profile of v1, /device:TPU:0, one launch (start us, length us, event | category | flops | bytes accessed | tf_op | source)
XLA Modules:
  0.0 133.1 jit_solution(4516848401133064484)
XLA Ops:
  0.0 10.3 %shard_map.84 = (f32[128,512]{1,0:T(8,128)}, f32[128,512]{1,0:T(8,128)}) custom-call(s32[1]{0:T(128)} %bitcast.8.core_ref, bf16[1024,7168]{1,0:T(8,128)(2,1)} %acts_ref.1, bf16[1024,2048]{1,0:T(8,128)(2,1)} %grads_ref.1, bf16[64,7168]{1,0:T(8,128)(2,1)} %bitcast.47, bf16[64,2048]{1,0:T(8,128)(2,1)} %bitcast.48), custom_call_target="tpu_custom_call" | custom-call | tf_op jit(solution)/shard_map/pallas_call | solution.py:179
  10.8 1.4 %collective-permute-done.36 = f32[128,512]{1,0:T(8,128)S(1)} collective-permute-done((f32[128,512]{1,0:T(8,128)}, f32[128,512]{1,0:T(8,128)S(1)}, u32[]{:S(2)}, u32[]{:S(2)}) %collective-permute-start.36) | collective-permute-done | bytes 262176 | tf_op jit(solution)/shard_map/ppermute | solution.py:153
  12.2 1.0 add.322
  13.2 2.9 %collective-permute-start.37 = (f32[96,512]{1,0:T(8,128)S(1)}, f32[96,512]{1,0:T(8,128)S(1)}, u32[]{:S(2)}, u32[]{:S(2)}) collective-permute-start(f32[96,512]{1,0:T(8,128)S(1)} %pad_maximum_fusion), channel_id=1, source_target_pairs={{0,2},{1,3},{2,0},{3,1},{4,6},{5,7},{6,4},{7,5},{8,10},{9,11},{10,... | collective-permute-start | bytes 589832 | tf_op jit(solution)/shard_map/ppermute | solution.py:153
  16.2 5.1 %collective-permute-done.37 = f32[96,512]{1,0:T(8,128)S(1)} collective-permute-done((f32[96,512]{1,0:T(8,128)S(1)}, f32[96,512]{1,0:T(8,128)S(1)}, u32[]{:S(2)}, u32[]{:S(2)}) %collective-permute-start.37) | collective-permute-done | bytes 196640 | tf_op jit(solution)/shard_map/ppermute | solution.py:153
  21.4 0.7 collective-permute-start.38
  22.1 3.2 %collective-permute-start.39 = (f32[104,512]{1,0:T(8,128)S(1)}, f32[104,512]{1,0:T(8,128)S(1)}, u32[]{:S(2)}, u32[]{:S(2)}) collective-permute-start(f32[104,512]{1,0:T(8,128)S(1)} %pad_maximum_fusion.2.refs_0_), channel_id=1, source_target_pairs={{0,1},{1,0},{2,3},{3,2},{4,5},{5,4},{6,7},{7,6},{8,9},{9,8},{10,11... | collective-permute-start | bytes 638984 | tf_op jit(solution)/shard_map/ppermute | solution.py:153
  25.3 5.0 %collective-permute-start.40 = (f32[104,512]{1,0:T(8,128)S(1)}, f32[104,512]{1,0:T(8,128)S(1)}, u32[]{:S(2)}, u32[]{:S(2)}) collective-permute-start(f32[104,512]{1,0:T(8,128)S(1)} %collective-permute-done.38.refs_1_), channel_id=1, source_target_pairs={{0,1},{1,0},{2,3},{3,2},{4,5},{5,4},{6,7},{7,6},{8,9},{9,8},{10,11... | collective-permute-start | bytes 638984 | tf_op jit(solution)/shard_map/ppermute | solution.py:153
  30.3 1.0 collective-permute-done.40.refs_3_
  31.3 9.3 %shard_map.85 = (f32[64,4096]{1,0:T(8,128)S(1)}, f32[64,4096]{1,0:T(8,128)S(1)}) custom-call(s32[2]{0:T(128)S(1)} %pad_add_fusion.1.first_ref, f32[104,512]{1,0:T(8,128)S(1)} %pad_maximum_fusion.2.refs_0_, f32[104,512]{1,0:T(8,128)S(1)} %collective-permute-done.38.refs_1_, f32[104,512]{1,0:T(8,128)S(1)} %collective-permute-done.39.refs_2_, ...), custom_call_target="tpu_custom_call" | custom-call | tf_op jit(solution)/shard_map/pallas_call | solution.py:216
  41.1 2.3 %collective-permute-done.41 = f32[64,4096]{1,0:T(8,128)S(1)} collective-permute-done((f32[64,4096]{1,0:T(8,128)S(1)}, f32[64,4096]{1,0:T(8,128)S(1)}, u32[]{:S(2)}, u32[]{:S(2)}) %collective-permute-start.41) | collective-permute-done | bytes 1048608 | tf_op jit(solution)/shard_map/ppermute | solution.py:153
  44.0 1.6 %collective-permute-start.43 = (f32[32,128]{0,1:T(8,128)S(1)}, f32[32,128]{0,1:T(8,128)S(1)}, u32[]{:S(2)}, u32[]{:S(2)}) collective-permute-start(f32[32,128]{0,1:T(8,128)S(1)} %broadcast_in_dim.49), channel_id=1, source_target_pairs={{0,2},{1,3},{2,0},{3,1},{4,6},{5,7},{6,4},{7,5},{8,10},{9,11},{10,... | collective-permute-start | bytes 49160 | tf_op jit(solution)/shard_map/ppermute | solution.py:153
  46.1 0.6 fusion.4
  49.1 4.9 %collective-permute-done.42 = f16[32,4096]{1,0:T(8,128)(2,1)S(1)} collective-permute-done((f16[32,4096]{1,0:T(8,128)(2,1)S(1)}, f16[32,4096]{1,0:T(8,128)(2,1)S(1)}, u32[]{:S(2)}, u32[]{:S(2)}) %collective-permute-start.42) | collective-permute-done | bytes 262176 | tf_op jit(solution)/shard_map/ppermute | solution.py:153
  54.2 1.6 %collective-permute-start.54 = (bf16[32,4096]{1,0:T(8,128)(2,1)S(1)}, bf16[32,4096]{1,0:T(8,128)(2,1)S(1)}, u32[]{:S(2)}, u32[]{:S(2)}) collective-permute-start(bf16[32,4096]{1,0:T(8,128)(2,1)S(1)} %select_convert_fusion.refs_0_), channel_id=1, source_target_pairs={{0,2},{1,5},{2,0},{3,7},{4,6},{5,1},{6,4},{7,3},{8,10},{9,13},{10,... | collective-permute-start | bytes 786440 | tf_op jit(solution)/shard_map/ppermute | solution.py:153
  55.8 1.5 %collective-permute-start.48 = (bf16[32,4096]{1,0:T(8,128)(2,1)S(1)}, bf16[32,4096]{1,0:T(8,128)(2,1)S(1)}, u32[]{:S(2)}, u32[]{:S(2)}) collective-permute-start(bf16[32,4096]{1,0:T(8,128)(2,1)S(1)} %collective-permute-done.47.refs_1_), channel_id=1, source_target_pairs={{0,2},{1,5},{2,0},{3,7},{4,6},{5,1},{6,4},{7,3},{8,10},{9,13},{10,... | collective-permute-start | bytes 786440 | tf_op jit(solution)/shard_map/ppermute | solution.py:153
  57.2 2.3 %collective-permute-start.44 = (bf16[32,4096]{1,0:T(8,128)(2,1)S(1)}, bf16[32,4096]{1,0:T(8,128)(2,1)S(1)}, u32[]{:S(2)}, u32[]{:S(2)}) collective-permute-start(bf16[32,4096]{1,0:T(8,128)(2,1)S(1)} %select_convert_fusion.refs_0_), channel_id=1, source_target_pairs={{0,8},{1,25},{2,10},{3,27},{4,12},{5,29},{6,14},{7,31},{8,16},{9,1... | collective-permute-start | bytes 786440 | tf_op jit(solution)/shard_map/ppermute | solution.py:153
  59.6 1.1 collective-permute-done.54.refs_2_
  61.1 1.9 %collective-permute-start.57 = (bf16[32,4096]{1,0:T(8,128)(2,1)S(1)}, bf16[32,4096]{1,0:T(8,128)(2,1)S(1)}, u32[]{:S(2)}, u32[]{:S(2)}) collective-permute-start(bf16[32,4096]{1,0:T(8,128)(2,1)S(1)} %collective-permute-done.47.refs_1_), channel_id=1, source_target_pairs={{0,8},{1,25},{2,10},{3,27},{4,12},{5,29},{6,14},{7,31},{8,16},{9,1... | collective-permute-start | bytes 786440 | tf_op jit(solution)/shard_map/ppermute | solution.py:153
  63.5 1.8 %collective-permute-start.49 = (bf16[32,4096]{1,0:T(8,128)(2,1)S(1)}, bf16[32,4096]{1,0:T(8,128)(2,1)S(1)}, u32[]{:S(2)}, u32[]{:S(2)}) collective-permute-start(bf16[32,4096]{1,0:T(8,128)(2,1)S(1)} %collective-permute-done.48.refs_3_), channel_id=1, source_target_pairs={{0,1},{1,0},{2,3},{3,2},{4,5},{5,4},{6,7},{7,6},{8,9},{9,8},{10,11... | collective-permute-start | bytes 786440 | tf_op jit(solution)/shard_map/ppermute | solution.py:153
  65.3 0.7 copy-done
  66.0 2.8 %collective-permute-done.44.refs_0_ = bf16[32,4096]{1,0:T(8,128)(2,1)S(1)} collective-permute-done((bf16[32,4096]{1,0:T(8,128)(2,1)S(1)}, bf16[32,4096]{1,0:T(8,128)(2,1)S(1)}, u32[]{:S(2)}, u32[]{:S(2)}) %collective-permute-start.44) | collective-permute-done | bytes 262176 | tf_op jit(solution)/shard_map/ppermute | solution.py:153
  68.9 0.7 copy-done.2
  69.6 2.1 %collective-permute-start.45 = (bf16[32,4096]{1,0:T(8,128)(2,1)S(1)}, bf16[32,4096]{1,0:T(8,128)(2,1)S(1)}, u32[]{:S(2)}, u32[]{:S(2)}) collective-permute-start(bf16[32,4096]{1,0:T(8,128)(2,1)S(1)} %collective-permute-done.44.refs_0_), channel_id=1, source_target_pairs={{0,1},{1,0},{2,3},{3,2},{4,5},{5,4},{6,7},{7,6},{8,9},{9,8},{10,11... | collective-permute-start | bytes 786440 | tf_op jit(solution)/shard_map/ppermute | solution.py:153
  71.7 2.7 %collective-permute-done.57.refs_1_ = bf16[32,4096]{1,0:T(8,128)(2,1)S(1)} collective-permute-done((bf16[32,4096]{1,0:T(8,128)(2,1)S(1)}, bf16[32,4096]{1,0:T(8,128)(2,1)S(1)}, u32[]{:S(2)}, u32[]{:S(2)}) %collective-permute-start.57) | collective-permute-done | bytes 262176 | tf_op jit(solution)/shard_map/ppermute | solution.py:153
  74.5 0.7 copy-done.4
  75.2 1.9 %collective-permute-start.59 = (bf16[32,4096]{1,0:T(8,128)(2,1)S(1)}, bf16[32,4096]{1,0:T(8,128)(2,1)S(1)}, u32[]{:S(2)}, u32[]{:S(2)}) collective-permute-start(bf16[32,4096]{1,0:T(8,128)(2,1)S(1)} %collective-permute-done.57.refs_1_), channel_id=1, source_target_pairs={{0,2},{1,5},{2,0},{3,7},{4,6},{5,1},{6,4},{7,3},{8,10},{9,13},{10,... | collective-permute-start | bytes 786440 | tf_op jit(solution)/shard_map/ppermute | solution.py:153
  77.1 2.6 %collective-permute-done.46.refs_0_ = bf16[32,4096]{1,0:T(8,128)(2,1)S(1)} collective-permute-done((bf16[32,4096]{1,0:T(8,128)(2,1)S(1)}, bf16[32,4096]{1,0:T(8,128)(2,1)S(1)}, u32[]{:S(2)}, u32[]{:S(2)}) %collective-permute-start.46) | collective-permute-done | bytes 262176 | tf_op jit(solution)/shard_map/ppermute | solution.py:153
  79.7 0.8 collective-permute-start.70
  80.6 1.2 collective-permute-start.60
  82.1 1.5 %collective-permute-done.59.refs_3_ = bf16[32,4096]{1,0:T(8,128)(2,1)S(1)} collective-permute-done((bf16[32,4096]{1,0:T(8,128)(2,1)S(1)}, bf16[32,4096]{1,0:T(8,128)(2,1)S(1)}, u32[]{:S(2)}, u32[]{:S(2)}) %collective-permute-start.59) | collective-permute-done | bytes 262176 | tf_op jit(solution)/shard_map/ppermute | solution.py:153
  83.8 2.7 %collective-permute-done.70.refs_2_ = bf16[32,4096]{1,0:T(8,128)(2,1)} collective-permute-done((bf16[32,4096]{1,0:T(8,128)(2,1)S(1)}, bf16[32,4096]{1,0:T(8,128)(2,1)}, u32[]{:S(2)}, u32[]{:S(2)}) %collective-permute-start.70) | collective-permute-done | bytes 262176 | tf_op jit(solution)/shard_map/ppermute | solution.py:153
  87.0 2.1 %collective-permute-done.60.refs_2_ = bf16[32,4096]{1,0:T(8,128)(2,1)S(1)} collective-permute-done((bf16[32,4096]{1,0:T(8,128)(2,1)S(1)}, bf16[32,4096]{1,0:T(8,128)(2,1)S(1)}, u32[]{:S(2)}, u32[]{:S(2)}) %collective-permute-start.60) | collective-permute-done | bytes 262176 | tf_op jit(solution)/shard_map/ppermute | solution.py:153
  89.3 2.0 %collective-permute-done.51.refs_6_ = bf16[32,4096]{1,0:T(8,128)(2,1)S(1)} collective-permute-done((bf16[32,4096]{1,0:T(8,128)(2,1)S(1)}, bf16[32,4096]{1,0:T(8,128)(2,1)S(1)}, u32[]{:S(2)}, u32[]{:S(2)}) %collective-permute-start.51) | collective-permute-done | bytes 262176 | tf_op jit(solution)/shard_map/ppermute | solution.py:153
  91.3 0.8 collective-permute-done.63.refs_3_
  92.1 0.6 collective-permute-start.52
  92.7 0.7 select_reduce_fusion
  93.5 1.4 %collective-permute-done.71.refs_3_ = bf16[32,4096]{1,0:T(8,128)(2,1)} collective-permute-done((bf16[32,4096]{1,0:T(8,128)(2,1)}, bf16[32,4096]{1,0:T(8,128)(2,1)}, u32[]{:S(2)}, u32[]{:S(2)}) %collective-permute-start.71) | collective-permute-done | bytes 262176 | tf_op jit(solution)/shard_map/ppermute | solution.py:153
  94.9 0.9 copy-done.1
  95.9 0.9 copy-done.3
  96.8 0.9 copy-done.5
  97.8 5.8 %shard_map.86 = f32[256,1024]{1,0:T(8,128)S(1)} custom-call(bf16[32,4096]{1,0:T(8,128)(2,1)S(1)} %select_convert_fusion.refs_0_, bf16[32,4096]{1,0:T(8,128)(2,1)S(1)} %collective-permute-done.47.refs_1_, bf16[32,4096]{1,0:T(8,128)(2,1)S(1)} %collective-permute-done.54.refs_2_, bf16[32,4096]{1,0:T(8,128)(2,1)S(1)} %copy-done.1, ...), custom_call_target="tpu_custom_call" | custom-call | flops 2147483648 | bytes 9437184 | tf_op jit(solution)/shard_map/pallas_call | solution.py:314
  103.6 2.3 %collective-permute-start.73 = (bf16[32,4096]{1,0:T(8,128)(2,1)}, bf16[32,4096]{1,0:T(8,128)(2,1)S(1)}, u32[]{:S(2)}, u32[]{:S(2)}) collective-permute-start(bf16[32,4096]{1,0:T(8,128)(2,1)} %collective-permute-done.71.refs_3_), channel_id=1, source_target_pairs={{0,1},{1,0},{2,3},{3,2},{4,5},{5,4},{6,7},{7,6},{8,9},{9,8},{10,11... | collective-permute-start | bytes 786440 | tf_op jit(solution)/shard_map/ppermute | solution.py:153
  107.0 5.7 %shard_map.87 = f32[256,1024]{1,0:T(8,128)S(1)} custom-call(bf16[32,4096]{1,0:T(8,128)(2,1)S(1)} %collective-permute-done.44.refs_0_, bf16[32,4096]{1,0:T(8,128)(2,1)S(1)} %collective-permute-done.57.refs_1_, bf16[32,4096]{1,0:T(8,128)(2,1)S(1)} %collective-permute-done.58.refs_2_, bf16[32,4096]{1,0:T(8,128)(2,1)S(1)} %collective-permute-done.59.refs_3_, ...), custom_call_target="tpu_custom_call" | custom-call | flops 2147483648 | bytes 9437184 | tf_op jit(solution)/shard_map/pallas_call | solution.py:314
  114.6 6.1 %shard_map.89 = f32[256,1024]{1,0:T(8,128)S(1)} custom-call(bf16[32,4096]{1,0:T(8,128)(2,1)S(1)} %collective-permute-done.46.refs_0_, bf16[32,4096]{1,0:T(8,128)(2,1)} %collective-permute-done.69.refs_1_, bf16[32,4096]{1,0:T(8,128)(2,1)} %collective-permute-done.70.refs_2_, bf16[32,4096]{1,0:T(8,128)(2,1)} %collective-permute-done.71.refs_3_, ...), custom_call_target="tpu_custom_call" | custom-call | flops 2147483648 | bytes 9437184 | tf_op jit(solution)/shard_map/pallas_call | solution.py:314
  120.8 5.9 %shard_map.88 = f32[256,1024]{1,0:T(8,128)S(1)} custom-call(bf16[32,4096]{1,0:T(8,128)(2,1)S(1)} %collective-permute-done.45.refs_0_, bf16[32,4096]{1,0:T(8,128)(2,1)S(1)} %collective-permute-done.62.refs_1_, bf16[32,4096]{1,0:T(8,128)(2,1)S(1)} %collective-permute-done.60.refs_2_, bf16[32,4096]{1,0:T(8,128)(2,1)} %collective-permute-done.63.refs_3_, ...), custom_call_target="tpu_custom_call" | custom-call | flops 2147483648 | bytes 9437184 | tf_op jit(solution)/shard_map/pallas_call | solution.py:314
  126.7 6.4 %conditional.1 = (f32[1024,1024]{1,0:T(8,128)}) conditional(s32[]{:T(128)} %bitcast.12, (s32[1024]{0:T(1024)S(1)}, f32[256,1024]{1,0:T(8,128)S(1)}, f32[256,1024]{1,0:T(8,128)S(1)}, f32[256,1024]{1,0:T(8,128)S(1)}, f32[256,1024]{1,0:T(8,128)S(1)}) %tuple.22, (s32[]{:T(128)}, s32[]{:T(128)}, f32[104,512]{1,0:T(8,128)S(1)}, f32[104,512]{1,0:T(8,128)S(1)}, ...), branch_computations={%region_2.3_spmd, %region_3.7_spmd} | conditional | flops 8591769600 | bytes 89934656 | solution.py:366
  126.7 6.4 %branch_0_fun.1 = f32[1024,1024]{1,0:T(8,128)} custom-call(s32[1024]{0:T(1024)S(1)} %get-tuple-element.116.dest_ref, f32[256,1024]{1,0:T(8,128)S(1)} %get-tuple-element.117.refs_0_, f32[256,1024]{1,0:T(8,128)S(1)} %get-tuple-element.118.refs_1_, f32[256,1024]{1,0:T(8,128)S(1)} %get-tuple-element.119.refs_2_, f32[256,1024]{1,0:T(8,128)S(1)} %get-tuple-element.120.refs_3_), custom_call_target="tpu_custom_call" | custom-call | tf_op jit(solution)/shard_map/cond/branch_0_fun/pallas_call | solution.py:329
  (86 shorter events, 6.7 us)
Async XLA Ops:
  0.0 16.1 %copy-start.10 = (s32[1024]{0:T(1024)S(1)}, s32[1024]{0:T(1024)}, u32[]{:S(2)}) copy-start(s32[1024]{0:T(1024)} %param.16) | copy-start | bytes 12292
  10.3 1.9 %collective-permute-start.36 = (f32[128,512]{1,0:T(8,128)}, f32[128,512]{1,0:T(8,128)S(1)}, u32[]{:S(2)}, u32[]{:S(2)}) collective-permute-start(f32[128,512]{1,0:T(8,128)} %get-tuple-element.148), channel_id=1, source_target_pairs={{0,1},{1,0},{2,3},{3,2},{4,5},{5,4},{6,7},{7,6},{8,9},{9,8},{10,11... | collective-permute-start | bytes 786440 | tf_op jit(solution)/shard_map/ppermute | solution.py:153
  13.2 8.1 %collective-permute-start.37 = (f32[96,512]{1,0:T(8,128)S(1)}, f32[96,512]{1,0:T(8,128)S(1)}, u32[]{:S(2)}, u32[]{:S(2)}) collective-permute-start(f32[96,512]{1,0:T(8,128)S(1)} %pad_maximum_fusion), channel_id=1, source_target_pairs={{0,2},{1,3},{2,0},{3,1},{4,6},{5,7},{6,4},{7,5},{8,10},{9,11},{10,... | collective-permute-start | bytes 589832 | tf_op jit(solution)/shard_map/ppermute | solution.py:153
  21.4 19.3 %copy-start.6 = (f32[104,512]{1,0:T(8,128)}, f32[104,512]{1,0:T(8,128)S(1)}, u32[]{:S(2)}) copy-start(f32[104,512]{1,0:T(8,128)S(1)} %pad_maximum_fusion.2.refs_0_) | copy-start | bytes 638980
  21.4 3.9 %collective-permute-start.38 = (f32[104,512]{1,0:T(8,128)S(1)}, f32[104,512]{1,0:T(8,128)S(1)}, u32[]{:S(2)}, u32[]{:S(2)}) collective-permute-start(f32[104,512]{1,0:T(8,128)S(1)} %pad_maximum_fusion.2.refs_0_), channel_id=1, source_target_pairs={{1,4},{3,6},{4,1},{5,8},{6,3},{7,10},{8,5},{9,12},{10,7},{11,14},{... | collective-permute-start | bytes 638984 | tf_op jit(solution)/shard_map/ppermute | solution.py:153
  22.1 8.2 %collective-permute-start.39 = (f32[104,512]{1,0:T(8,128)S(1)}, f32[104,512]{1,0:T(8,128)S(1)}, u32[]{:S(2)}, u32[]{:S(2)}) collective-permute-start(f32[104,512]{1,0:T(8,128)S(1)} %pad_maximum_fusion.2.refs_0_), channel_id=1, source_target_pairs={{0,1},{1,0},{2,3},{3,2},{4,5},{5,4},{6,7},{7,6},{8,9},{9,8},{10,11... | collective-permute-start | bytes 638984 | tf_op jit(solution)/shard_map/ppermute | solution.py:153
  25.3 6.1 %collective-permute-start.40 = (f32[104,512]{1,0:T(8,128)S(1)}, f32[104,512]{1,0:T(8,128)S(1)}, u32[]{:S(2)}, u32[]{:S(2)}) collective-permute-start(f32[104,512]{1,0:T(8,128)S(1)} %collective-permute-done.38.refs_1_), channel_id=1, source_target_pairs={{0,1},{1,0},{2,3},{3,2},{4,5},{5,4},{6,7},{7,6},{8,9},{9,8},{10,11... | collective-permute-start | bytes 638984 | tf_op jit(solution)/shard_map/ppermute | solution.py:153
  30.3 10.3 %copy-start.8 = (f32[104,512]{1,0:T(8,128)}, f32[104,512]{1,0:T(8,128)S(1)}, u32[]{:S(2)}) copy-start(f32[104,512]{1,0:T(8,128)S(1)} %collective-permute-done.39.refs_2_) | copy-start | bytes 638980
  40.7 52.1 %copy-start.11 = (s32[1024]{0:T(1024)S(1)}, s32[1024]{0:T(1024)}, u32[]{:S(2)}) copy-start(s32[1024]{0:T(1024)} %param.17) | copy-start | bytes 12292
  40.7 2.7 %collective-permute-start.41 = (f32[64,4096]{1,0:T(8,128)S(1)}, f32[64,4096]{1,0:T(8,128)S(1)}, u32[]{:S(2)}, u32[]{:S(2)}) collective-permute-start(f32[64,4096]{1,0:T(8,128)S(1)} %get-tuple-element.150), channel_id=1, source_target_pairs={{0,1},{1,0},{2,3},{3,2},{4,5},{5,4},{6,7},{7,6},{8,9},{9,8},{10,11... | collective-permute-start | bytes 3145736 | tf_op jit(solution)/shard_map/ppermute | solution.py:153
  44.0 5.2 %collective-permute-start.43 = (f32[32,128]{0,1:T(8,128)S(1)}, f32[32,128]{0,1:T(8,128)S(1)}, u32[]{:S(2)}, u32[]{:S(2)}) collective-permute-start(f32[32,128]{0,1:T(8,128)S(1)} %broadcast_in_dim.49), channel_id=1, source_target_pairs={{0,2},{1,3},{2,0},{3,1},{4,6},{5,7},{6,4},{7,5},{8,10},{9,11},{10,... | collective-permute-start | bytes 49160 | tf_op jit(solution)/shard_map/ppermute | solution.py:153
  45.5 8.5 %collective-permute-start.42 = (f16[32,4096]{1,0:T(8,128)(2,1)S(1)}, f16[32,4096]{1,0:T(8,128)(2,1)S(1)}, u32[]{:S(2)}, u32[]{:S(2)}) collective-permute-start(f16[32,4096]{1,0:T(8,128)(2,1)S(1)} %divide_convert_fusion.1), channel_id=1, source_target_pairs={{0,2},{1,3},{2,0},{3,1},{4,6},{5,7},{6,4},{7,5},{8,10},{9,11},{10,... | collective-permute-start | bytes 786440 | tf_op jit(solution)/shard_map/ppermute | solution.py:153
  54.2 1.6 %collective-permute-start.47 = (bf16[32,4096]{1,0:T(8,128)(2,1)S(1)}, bf16[32,4096]{1,0:T(8,128)(2,1)S(1)}, u32[]{:S(2)}, u32[]{:S(2)}) collective-permute-start(bf16[32,4096]{1,0:T(8,128)(2,1)S(1)} %select_convert_fusion.refs_0_), channel_id=1, source_target_pairs={{0,1},{1,0},{2,3},{3,2},{4,5},{5,4},{6,7},{7,6},{8,9},{9,8},{10,11... | collective-permute-start | bytes 786440 | tf_op jit(solution)/shard_map/ppermute | solution.py:153
  54.2 6.4 %collective-permute-start.54 = (bf16[32,4096]{1,0:T(8,128)(2,1)S(1)}, bf16[32,4096]{1,0:T(8,128)(2,1)S(1)}, u32[]{:S(2)}, u32[]{:S(2)}) collective-permute-start(bf16[32,4096]{1,0:T(8,128)(2,1)S(1)} %select_convert_fusion.refs_0_), channel_id=1, source_target_pairs={{0,2},{1,5},{2,0},{3,7},{4,6},{5,1},{6,4},{7,3},{8,10},{9,13},{10,... | collective-permute-start | bytes 786440 | tf_op jit(solution)/shard_map/ppermute | solution.py:153
  55.8 7.7 %collective-permute-start.48 = (bf16[32,4096]{1,0:T(8,128)(2,1)S(1)}, bf16[32,4096]{1,0:T(8,128)(2,1)S(1)}, u32[]{:S(2)}, u32[]{:S(2)}) collective-permute-start(bf16[32,4096]{1,0:T(8,128)(2,1)S(1)} %collective-permute-done.47.refs_1_), channel_id=1, source_target_pairs={{0,2},{1,5},{2,0},{3,7},{4,6},{5,1},{6,4},{7,3},{8,10},{9,13},{10,... | collective-permute-start | bytes 786440 | tf_op jit(solution)/shard_map/ppermute | solution.py:153
  57.2 11.5 %collective-permute-start.44 = (bf16[32,4096]{1,0:T(8,128)(2,1)S(1)}, bf16[32,4096]{1,0:T(8,128)(2,1)S(1)}, u32[]{:S(2)}, u32[]{:S(2)}) collective-permute-start(bf16[32,4096]{1,0:T(8,128)(2,1)S(1)} %select_convert_fusion.refs_0_), channel_id=1, source_target_pairs={{0,8},{1,25},{2,10},{3,27},{4,12},{5,29},{6,14},{7,31},{8,16},{9,1... | collective-permute-start | bytes 786440 | tf_op jit(solution)/shard_map/ppermute | solution.py:153
  60.7 8.2 %collective-permute-start.55 = (bf16[32,4096]{1,0:T(8,128)(2,1)S(1)}, bf16[32,4096]{1,0:T(8,128)(2,1)S(1)}, u32[]{:S(2)}, u32[]{:S(2)}) collective-permute-start(bf16[32,4096]{1,0:T(8,128)(2,1)S(1)} %collective-permute-done.54.refs_2_), channel_id=1, source_target_pairs={{0,1},{1,0},{2,3},{3,2},{4,5},{5,4},{6,7},{7,6},{8,9},{9,8},{10,11... | collective-permute-start | bytes 786440 | tf_op jit(solution)/shard_map/ppermute | solution.py:153
  61.1 13.2 %collective-permute-start.57 = (bf16[32,4096]{1,0:T(8,128)(2,1)S(1)}, bf16[32,4096]{1,0:T(8,128)(2,1)S(1)}, u32[]{:S(2)}, u32[]{:S(2)}) collective-permute-start(bf16[32,4096]{1,0:T(8,128)(2,1)S(1)} %collective-permute-done.47.refs_1_), channel_id=1, source_target_pairs={{0,8},{1,25},{2,10},{3,27},{4,12},{5,29},{6,14},{7,31},{8,16},{9,1... | collective-permute-start | bytes 786440 | tf_op jit(solution)/shard_map/ppermute | solution.py:153
  63.5 10.9 %collective-permute-start.49 = (bf16[32,4096]{1,0:T(8,128)(2,1)S(1)}, bf16[32,4096]{1,0:T(8,128)(2,1)S(1)}, u32[]{:S(2)}, u32[]{:S(2)}) collective-permute-start(bf16[32,4096]{1,0:T(8,128)(2,1)S(1)} %collective-permute-done.48.refs_3_), channel_id=1, source_target_pairs={{0,1},{1,0},{2,3},{3,2},{4,5},{5,4},{6,7},{7,6},{8,9},{9,8},{10,11... | collective-permute-start | bytes 786440 | tf_op jit(solution)/shard_map/ppermute | solution.py:153
  68.8 6.4 %collective-permute-start.58 = (bf16[32,4096]{1,0:T(8,128)(2,1)S(1)}, bf16[32,4096]{1,0:T(8,128)(2,1)S(1)}, u32[]{:S(2)}, u32[]{:S(2)}) collective-permute-start(bf16[32,4096]{1,0:T(8,128)(2,1)S(1)} %collective-permute-done.44.refs_0_), channel_id=1, source_target_pairs={{0,2},{1,5},{2,0},{3,7},{4,6},{5,1},{6,4},{7,3},{8,10},{9,13},{10,... | collective-permute-start | bytes 786440 | tf_op jit(solution)/shard_map/ppermute | solution.py:153
  68.9 10.8 %collective-permute-start.46 = (bf16[32,4096]{1,0:T(8,128)(2,1)S(1)}, bf16[32,4096]{1,0:T(8,128)(2,1)S(1)}, u32[]{:S(2)}, u32[]{:S(2)}) collective-permute-start(bf16[32,4096]{1,0:T(8,128)(2,1)S(1)} %collective-permute-done.44.refs_0_), channel_id=1, source_target_pairs={{0,8},{1,25},{2,10},{3,27},{4,12},{5,29},{6,14},{7,31},{8,16},{9,1... | collective-permute-start | bytes 786440 | tf_op jit(solution)/shard_map/ppermute | solution.py:153
  69.6 11.0 %collective-permute-start.45 = (bf16[32,4096]{1,0:T(8,128)(2,1)S(1)}, bf16[32,4096]{1,0:T(8,128)(2,1)S(1)}, u32[]{:S(2)}, u32[]{:S(2)}) collective-permute-start(bf16[32,4096]{1,0:T(8,128)(2,1)S(1)} %collective-permute-done.44.refs_0_), channel_id=1, source_target_pairs={{0,1},{1,0},{2,3},{3,2},{4,5},{5,4},{6,7},{7,6},{8,9},{9,8},{10,11... | collective-permute-start | bytes 786440 | tf_op jit(solution)/shard_map/ppermute | solution.py:153
  74.4 6.2 %collective-permute-start.62 = (bf16[32,4096]{1,0:T(8,128)(2,1)S(1)}, bf16[32,4096]{1,0:T(8,128)(2,1)S(1)}, u32[]{:S(2)}, u32[]{:S(2)}) collective-permute-start(bf16[32,4096]{1,0:T(8,128)(2,1)S(1)} %collective-permute-done.57.refs_1_), channel_id=1, source_target_pairs={{0,1},{1,0},{2,3},{3,2},{4,5},{5,4},{6,7},{7,6},{8,9},{9,8},{10,11... | collective-permute-start | bytes 786440 | tf_op jit(solution)/shard_map/ppermute | solution.py:153
  74.4 7.4 %collective-permute-start.50 = (bf16[32,4096]{1,0:T(8,128)(2,1)S(1)}, bf16[32,4096]{1,0:T(8,128)(2,1)S(1)}, u32[]{:S(2)}, u32[]{:S(2)}) collective-permute-start(bf16[32,4096]{1,0:T(8,128)(2,1)S(1)} %collective-permute-done.49.refs_5_), channel_id=1, source_target_pairs={{0,2},{1,5},{2,0},{3,7},{4,6},{5,1},{6,4},{7,3},{8,10},{9,13},{10,... | collective-permute-start | bytes 786440 | tf_op jit(solution)/shard_map/ppermute | solution.py:153
  75.2 8.4 %collective-permute-start.59 = (bf16[32,4096]{1,0:T(8,128)(2,1)S(1)}, bf16[32,4096]{1,0:T(8,128)(2,1)S(1)}, u32[]{:S(2)}, u32[]{:S(2)}) collective-permute-start(bf16[32,4096]{1,0:T(8,128)(2,1)S(1)} %collective-permute-done.57.refs_1_), channel_id=1, source_target_pairs={{0,2},{1,5},{2,0},{3,7},{4,6},{5,1},{6,4},{7,3},{8,10},{9,13},{10,... | collective-permute-start | bytes 786440 | tf_op jit(solution)/shard_map/ppermute | solution.py:153
  79.7 6.8 %collective-permute-start.70 = (bf16[32,4096]{1,0:T(8,128)(2,1)S(1)}, bf16[32,4096]{1,0:T(8,128)(2,1)}, u32[]{:S(2)}, u32[]{:S(2)}) collective-permute-start(bf16[32,4096]{1,0:T(8,128)(2,1)S(1)} %collective-permute-done.46.refs_0_), channel_id=1, source_target_pairs={{0,2},{1,5},{2,0},{3,7},{4,6},{5,1},{6,4},{7,3},{8,10},{9,13},{10,... | collective-permute-start | bytes 786440 | tf_op jit(solution)/shard_map/ppermute | solution.py:153
  80.6 5.9 %collective-permute-start.69 = (bf16[32,4096]{1,0:T(8,128)(2,1)S(1)}, bf16[32,4096]{1,0:T(8,128)(2,1)}, u32[]{:S(2)}, u32[]{:S(2)}) collective-permute-start(bf16[32,4096]{1,0:T(8,128)(2,1)S(1)} %collective-permute-done.46.refs_0_), channel_id=1, source_target_pairs={{0,1},{1,0},{2,3},{3,2},{4,5},{5,4},{6,7},{7,6},{8,9},{9,8},{10,11... | collective-permute-start | bytes 786440 | tf_op jit(solution)/shard_map/ppermute | solution.py:153
  80.6 8.6 %collective-permute-start.60 = (bf16[32,4096]{1,0:T(8,128)(2,1)S(1)}, bf16[32,4096]{1,0:T(8,128)(2,1)S(1)}, u32[]{:S(2)}, u32[]{:S(2)}) collective-permute-start(bf16[32,4096]{1,0:T(8,128)(2,1)S(1)} %collective-permute-done.45.refs_0_), channel_id=1, source_target_pairs={{0,2},{1,5},{2,0},{3,7},{4,6},{5,1},{6,4},{7,3},{8,10},{9,13},{10,... | collective-permute-start | bytes 786440 | tf_op jit(solution)/shard_map/ppermute | solution.py:153
  81.8 9.5 %collective-permute-start.51 = (bf16[32,4096]{1,0:T(8,128)(2,1)S(1)}, bf16[32,4096]{1,0:T(8,128)(2,1)S(1)}, u32[]{:S(2)}, u32[]{:S(2)}) collective-permute-start(bf16[32,4096]{1,0:T(8,128)(2,1)S(1)} %collective-permute-done.50.refs_6_), channel_id=1, source_target_pairs={{0,8},{1,25},{2,10},{3,27},{4,12},{5,29},{6,14},{7,31},{8,16},{9,1... | collective-permute-start | bytes 786440 | tf_op jit(solution)/shard_map/ppermute | solution.py:153
  83.6 8.5 %collective-permute-start.63 = (bf16[32,4096]{1,0:T(8,128)(2,1)S(1)}, bf16[32,4096]{1,0:T(8,128)(2,1)}, u32[]{:S(2)}, u32[]{:S(2)}) collective-permute-start(bf16[32,4096]{1,0:T(8,128)(2,1)S(1)} %collective-permute-done.62.refs_1_), channel_id=1, source_target_pairs={{0,2},{1,5},{2,0},{3,7},{4,6},{5,1},{6,4},{7,3},{8,10},{9,13},{10,... | collective-permute-start | bytes 786440 | tf_op jit(solution)/shard_map/ppermute | solution.py:153
  86.5 7.0 %collective-permute-start.72 = (bf16[32,4096]{1,0:T(8,128)(2,1)}, bf16[32,4096]{1,0:T(8,128)(2,1)}, u32[]{:S(2)}, u32[]{:S(2)}) collective-permute-start(bf16[32,4096]{1,0:T(8,128)(2,1)} %collective-permute-done.70.refs_2_), channel_id=1, source_target_pairs={{0,1},{1,0},{2,3},{3,2},{4,5},{5,4},{6,7},{7,6},{8,9},{9,8},{10,11... | collective-permute-start | bytes 786440 | tf_op jit(solution)/shard_map/ppermute | solution.py:153
  86.5 8.4 %collective-permute-start.71 = (bf16[32,4096]{1,0:T(8,128)(2,1)}, bf16[32,4096]{1,0:T(8,128)(2,1)}, u32[]{:S(2)}, u32[]{:S(2)}) collective-permute-start(bf16[32,4096]{1,0:T(8,128)(2,1)} %collective-permute-done.69.refs_1_), channel_id=1, source_target_pairs={{0,2},{1,5},{2,0},{3,7},{4,6},{5,1},{6,4},{7,3},{8,10},{9,13},{10,... | collective-permute-start | bytes 786440 | tf_op jit(solution)/shard_map/ppermute | solution.py:153
  89.2 5.7 %collective-permute-start.56 = (bf16[32,4096]{1,0:T(8,128)(2,1)S(1)}, bf16[32,4096]{1,0:T(8,128)(2,1)}, u32[]{:S(2)}, u32[]{:S(2)}) collective-permute-start(bf16[32,4096]{1,0:T(8,128)(2,1)S(1)} %collective-permute-done.50.refs_6_), channel_id=1, source_target_pairs={{0,1},{1,0},{2,3},{3,2},{4,5},{5,4},{6,7},{7,6},{8,9},{9,8},{10,11... | collective-permute-start | bytes 786440 | tf_op jit(solution)/shard_map/ppermute | solution.py:153
  91.3 12.3 %collective-permute-start.53 = (bf16[32,4096]{1,0:T(8,128)(2,1)S(1)}, bf16[32,4096]{1,0:T(8,128)(2,1)S(1)}, u32[]{:S(2)}, u32[]{:S(2)}) collective-permute-start(bf16[32,4096]{1,0:T(8,128)(2,1)S(1)} %collective-permute-done.51.refs_6_), channel_id=1, source_target_pairs={{0,8},{1,25},{2,10},{3,27},{4,12},{5,29},{6,14},{7,31},{8,16},{9,1... | collective-permute-start | bytes 786440 | tf_op jit(solution)/shard_map/ppermute | solution.py:153
  92.1 13.8 %collective-permute-start.52 = (bf16[32,4096]{1,0:T(8,128)(2,1)S(1)}, bf16[32,4096]{1,0:T(8,128)(2,1)S(1)}, u32[]{:S(2)}, u32[]{:S(2)}) collective-permute-start(bf16[32,4096]{1,0:T(8,128)(2,1)S(1)} %collective-permute-done.51.refs_6_), channel_id=1, source_target_pairs={{0,1},{1,0},{2,3},{3,2},{4,5},{5,4},{6,7},{7,6},{8,9},{9,8},{10,11... | collective-permute-start | bytes 786440 | tf_op jit(solution)/shard_map/ppermute | solution.py:153
  93.4 12.6 %collective-permute-start.61 = (bf16[32,4096]{1,0:T(8,128)(2,1)S(1)}, bf16[32,4096]{1,0:T(8,128)(2,1)S(1)}, u32[]{:S(2)}, u32[]{:S(2)}) collective-permute-start(bf16[32,4096]{1,0:T(8,128)(2,1)S(1)} %collective-permute-done.60.refs_2_), channel_id=1, source_target_pairs={{0,1},{1,0},{2,3},{3,2},{4,5},{5,4},{6,7},{7,6},{8,9},{9,8},{10,11... | collective-permute-start | bytes 786440 | tf_op jit(solution)/shard_map/ppermute | solution.py:153
  94.9 11.6 %collective-permute-start.64 = (bf16[32,4096]{1,0:T(8,128)(2,1)}, bf16[32,4096]{1,0:T(8,128)(2,1)S(1)}, u32[]{:S(2)}, u32[]{:S(2)}) collective-permute-start(bf16[32,4096]{1,0:T(8,128)(2,1)} %collective-permute-done.63.refs_3_), channel_id=1, source_target_pairs={{0,1},{1,0},{2,3},{3,2},{4,5},{5,4},{6,7},{7,6},{8,9},{9,8},{10,11... | collective-permute-start | bytes 786440 | tf_op jit(solution)/shard_map/ppermute | solution.py:153
  94.9 11.7 %collective-permute-start.65 = (bf16[32,4096]{1,0:T(8,128)(2,1)}, bf16[32,4096]{1,0:T(8,128)(2,1)S(1)}, u32[]{:S(2)}, u32[]{:S(2)}) collective-permute-start(bf16[32,4096]{1,0:T(8,128)(2,1)} %collective-permute-done.56.refs_7_), channel_id=1, source_target_pairs={{0,8},{1,25},{2,10},{3,27},{4,12},{5,29},{6,14},{7,31},{8,16},{9,1... | collective-permute-start | bytes 786440 | tf_op jit(solution)/shard_map/ppermute | solution.py:153
  94.9 1.0 copy-start.1
  95.9 0.9 copy-start.3
  96.8 0.9 copy-start.5
  103.6 11.0 %collective-permute-start.73 = (bf16[32,4096]{1,0:T(8,128)(2,1)}, bf16[32,4096]{1,0:T(8,128)(2,1)S(1)}, u32[]{:S(2)}, u32[]{:S(2)}) collective-permute-start(bf16[32,4096]{1,0:T(8,128)(2,1)} %collective-permute-done.71.refs_3_), channel_id=1, source_target_pairs={{0,1},{1,0},{2,3},{3,2},{4,5},{5,4},{6,7},{7,6},{8,9},{9,8},{10,11... | collective-permute-start | bytes 786440 | tf_op jit(solution)/shard_map/ppermute | solution.py:153
  105.9 8.7 %collective-permute-start.74 = (bf16[32,4096]{1,0:T(8,128)(2,1)S(1)}, bf16[32,4096]{1,0:T(8,128)(2,1)S(1)}, u32[]{:S(2)}, u32[]{:S(2)}) collective-permute-start(bf16[32,4096]{1,0:T(8,128)(2,1)S(1)} %collective-permute-done.53.refs_6_), channel_id=1, source_target_pairs={{0,1},{1,0},{2,3},{3,2},{4,5},{5,4},{6,7},{7,6},{8,9},{9,8},{10,11... | collective-permute-start | bytes 786440 | tf_op jit(solution)/shard_map/ppermute | solution.py:153
  106.0 14.7 %collective-permute-start.66 = (bf16[32,4096]{1,0:T(8,128)(2,1)S(1)}, bf16[32,4096]{1,0:T(8,128)(2,1)S(1)}, u32[]{:S(2)}, u32[]{:S(2)}) collective-permute-start(bf16[32,4096]{1,0:T(8,128)(2,1)S(1)} %collective-permute-done.58.refs_2_), channel_id=1, source_target_pairs={{0,1},{1,0},{2,3},{3,2},{4,5},{5,4},{6,7},{7,6},{8,9},{9,8},{10,11... | collective-permute-start | bytes 786440 | tf_op jit(solution)/shard_map/ppermute | solution.py:153
  106.5 14.2 %collective-permute-start.67 = (bf16[32,4096]{1,0:T(8,128)(2,1)S(1)}, bf16[32,4096]{1,0:T(8,128)(2,1)S(1)}, u32[]{:S(2)}, u32[]{:S(2)}) collective-permute-start(bf16[32,4096]{1,0:T(8,128)(2,1)S(1)} %collective-permute-done.59.refs_3_), channel_id=1, source_target_pairs={{0,1},{1,0},{2,3},{3,2},{4,5},{5,4},{6,7},{7,6},{8,9},{9,8},{10,11... | collective-permute-start | bytes 786440 | tf_op jit(solution)/shard_map/ppermute | solution.py:153
  106.6 14.1 %collective-permute-start.68 = (bf16[32,4096]{1,0:T(8,128)(2,1)S(1)}, bf16[32,4096]{1,0:T(8,128)(2,1)S(1)}, u32[]{:S(2)}, u32[]{:S(2)}) collective-permute-start(bf16[32,4096]{1,0:T(8,128)(2,1)S(1)} %collective-permute-done.65.refs_7_), channel_id=1, source_target_pairs={{0,1},{1,0},{2,3},{3,2},{4,5},{5,4},{6,7},{7,6},{8,9},{9,8},{10,11... | collective-permute-start | bytes 786440 | tf_op jit(solution)/shard_map/ppermute | solution.py:153
  120.7 6.0 %copy-start.7 = (f32[104,512]{1,0:T(8,128)S(1)}, f32[104,512]{1,0:T(8,128)}, u32[]{:S(2)}) copy-start(f32[104,512]{1,0:T(8,128)} %copy-done.6) | copy-start | bytes 638980
  120.7 6.0 %copy-start.9 = (f32[104,512]{1,0:T(8,128)S(1)}, f32[104,512]{1,0:T(8,128)}, u32[]{:S(2)}) copy-start(f32[104,512]{1,0:T(8,128)} %copy-done.8) | copy-start | bytes 638980
  (3 other events, 2.1 us)
